TPU v7x, 128 devices: a whole 4x4x4 slice. The times are simulated.
128 devices in a mesh: tx: 8 (over x, core), ty: 16 (over z, y).
Axes of the slice: x: 4, y: 4, z: 4, core: 2. Of those that a mesh axis runs over, the one named last changes fastest.
Arguments:
- solution: float32 [4, 1024, 4096], P(None, 'tx', 'ty'), may hold values from -6 to 6
- residual: float32 [4, 1024, 4096], P(None, 'tx', 'ty')
- direction: float32 [4, 1024, 4096], P(None, 'tx', 'ty')
- blocks: bfloat16 [32768, 128, 256], P(('tx', 'ty')), may hold values from -0.375 to 0.375
- bin_owner: int32 [32768, 1], P(('tx', 'ty')), may hold values from 0 to 127; in each aligned block of 256 rows (0 to 255, 256 to 511, ...) at most 3 rows name the same one
- bin_tile: int32 [32768], P(('tx', 'ty')), may hold values from 0 to 127
Outputs:
- next_solution: float32 [4, 1024, 4096], P(None, 'tx', 'ty')
- next_residual: float32 [4, 1024, 4096], P(None, 'tx', 'ty')
- next_direction: float32 [4, 1024, 4096], P(None, 'tx', 'ty')
Inputs may be any that keep to these rules, and one draw needn't show every extreme that they name: `bin_owner`: among the bins of one device, at most 3 name the same owner, and on some devices some owner is named by exactly 3 of them.
All inputs are finite; a program needn't handle non-finite values.
Results may differ from a plain program's by a relative error of at most 0.0024.
Values may be sent and summed in bfloat16 or wider, within the bound.
A program may use at most 128 MiB of HBM per device.

v0:
```python
import jax
import jax.numpy as jnp
from jax import lax
from jax.sharding import PartitionSpec as P

TILE_SIDE = 16


smooth_weight = 0.25


def padded_2(shard, sides, width):
    for axis, dim in sides:
        size, length = (lax.axis_size(axis), shard.shape[dim])
        up = [(i, (i + 1) % size) for i in range(size - 1)]
        down = [(j, i) for i, j in up]
        last = lax.slice_in_dim(shard, length - width, length, axis=dim)
        initial = lax.slice_in_dim(shard, 0, width, axis=dim)
        before = lax.ppermute(last, axis, up)
        after = lax.ppermute(initial, axis, down)
        shard = jnp.concatenate([before, shard, after], axis=dim)
    return shard


def to_tiles(field):
    beacons, rows, cols = field.shape
    across = rows // TILE_SIDE
    down = cols // TILE_SIDE
    shaped = field.reshape(beacons, across, TILE_SIDE, down, TILE_SIDE).transpose(1, 3, 0, 2, 4)
    return shaped.reshape(across * down, beacons, TILE_SIDE * TILE_SIDE)


def to_field(tiles, rows, cols):
    beacons = tiles.shape[1]
    across = rows // TILE_SIDE
    down = cols // TILE_SIDE
    shaped = tiles.reshape(across, down, beacons, TILE_SIDE, TILE_SIDE).transpose(2, 0, 3, 1, 4)
    return shaped.reshape(beacons, rows, cols)


def laplace_local(field):
    padded = padded_2(field.astype(jnp.bfloat16), (("tx", 1), ("ty", 2)), 1).astype(field.dtype)
    near = padded[:, 2:, 1:-1] + padded[:, :-2, 1:-1] + padded[:, 1:-1, 2:] + padded[:, 1:-1, :-2]
    return 4.0 * field - near


def per_device(solution, residual, direction, blocks, bin_owner, bin_tile):
    beacons, rows, cols = direction.shape
    cells = TILE_SIDE * TILE_SIDE
    across_x = lax.axis_size("tx")
    across_y = lax.axis_size("ty")
    devices = across_x * across_y
    count = blocks.shape[0]
    cap = max(2, 3 * count // (2 * devices))
    owner = bin_owner[:, 0]
    member = (owner[:, None] == jnp.arange(devices, dtype=jnp.int32)[None, :]).astype(jnp.int32)
    before = jnp.cumsum(member, axis=0) - member
    rank = jnp.sum(before * member, axis=1)
    slot = owner * cap + rank
    request = jnp.full((devices * cap,), -1, jnp.int32).at[slot].set(bin_tile)
    wanted = lax.all_to_all(
        request.reshape(devices, cap), ("tx", "ty"), split_axis=0, concat_axis=0, tiled=True
    )
    wanted = jnp.maximum(wanted.reshape(devices * cap), 0)
    own_tiles = to_tiles(direction.astype(jnp.bfloat16))
    outgoing = jnp.take(own_tiles, wanted, axis=0)
    fetched = lax.all_to_all(
        outgoing.reshape(devices, cap, beacons, cells),
        ("tx", "ty"),
        split_axis=0,
        concat_axis=0,
        tiled=True,
    )
    fetched = fetched.reshape(devices * cap, beacons, cells)
    picked = jnp.take(fetched, slot, axis=0)
    samples = jnp.einsum("bsc,bkc->bks", blocks, picked, preferred_element_type=jnp.float32).astype(
        jnp.bfloat16
    )
    adjoint = jnp.einsum("bsc,bks->bkc", blocks, samples, preferred_element_type=jnp.float32)
    returned = jnp.zeros((devices * cap, beacons, cells), jnp.float32).at[slot].set(adjoint)
    arrived = lax.all_to_all(
        returned.reshape(devices, cap, beacons, cells),
        ("tx", "ty"),
        split_axis=0,
        concat_axis=0,
        tiled=True,
    )
    arrived = arrived.reshape(devices * cap, beacons, cells)
    data_tiles = jnp.zeros(own_tiles.shape, jnp.float32).at[wanted].add(arrived)
    image = to_field(data_tiles, rows, cols) + smooth_weight * laplace_local(direction)
    norm_old = lax.psum(jnp.sum(residual * residual, axis=(1, 2)), ("tx", "ty"))
    curvature = lax.psum(jnp.sum(direction * image, axis=(1, 2)), ("tx", "ty"))
    alpha = norm_old / curvature
    next_residual = residual - alpha[:, None, None] * image
    norm_new = lax.psum(jnp.sum(next_residual * next_residual, axis=(1, 2)), ("tx", "ty"))
    next_solution = solution + alpha[:, None, None] * direction
    next_direction = next_residual + (norm_new / norm_old)[:, None, None] * direction
    return (next_solution, next_residual, next_direction)


def solution(mesh):
    placed = (
        P(None, "tx", "ty"),
        P(None, "tx", "ty"),
        P(None, "tx", "ty"),
        P(("tx", "ty"), None, None),
        P(("tx", "ty"), None),
        P(("tx", "ty")),
    )
    return jax.shard_map(
        per_device,
        mesh=mesh,
        in_specs=placed,
        out_specs=(P(None, "tx", "ty"), P(None, "tx", "ty"), P(None, "tx", "ty")),
        check_vma=False,
    )
```

profile of v0, /device:TPU:1, one launch (start us, length us, event | category | flops | bytes accessed | tf_op | source)
XLA Modules:
  0.0 293.8 jit_solution(3272720926653905522)
XLA Ops:
  0.6 0.8 copy.23
  1.7 0.9 fusion.12
  3.3 1.6 scatter_custom_fusion
  4.8 0.8 all_to_all.12
  5.7 11.5 %all-to-all-start = ((s32[128,1,3]{2,1,0:T(1,128)}), s32[128,1,3]{2,1,0:T(1,128)S(1)}, u32[]{:S(2)}, u32[]{:S(2)}) async-start(s32[128,1,3]{2,1,0:T(1,128)} %bitcast.7), calls=%async_computation | async-start | bytes 131072 | tf_op jit(solution)/shard_map/all_to_all | solution.py:61
  17.2 1.1 convert_element_type.19
  18.3 2.5 reshape.85
  20.7 2.1 copy.33
  22.9 2.0 reshape.86
  25.1 1.8 all-to-all-done
  27.7 2.3 gather_fusion
  30.0 1.4 broadcast_select_fusion
  31.4 8.0 %all-to-all-start.1 = ((bf16[128,3,4,256]{3,2,1,0:T(4,128)(2,1)}), bf16[128,3,4,256]{3,2,1,0:T(4,128)(2,1)S(1)}, u32[]{:S(2)}, u32[]{:S(2)}) async-start(bf16[128,3,4,256]{3,2,1,0:T(4,128)(2,1)} %broadcast_select_fusion), calls=%async_computation.1 | async-start | bytes 1572864 | tf_op jit(solution)/shard_map/all_to_all | solution.py:67
  39.5 16.6 %all-to-all-done.1 = bf16[128,3,4,256]{3,2,1,0:T(4,128)(2,1)S(1)} async-done(((bf16[128,3,4,256]{3,2,1,0:T(4,128)(2,1)}), bf16[128,3,4,256]{3,2,1,0:T(4,128)(2,1)S(1)}, u32[]{:S(2)}, u32[]{:S(2)}) %all-to-all-start.1) | async-done | bytes 786464 | tf_op jit(solution)/shard_map/all_to_all | solution.py:67
  56.1 1.2 gather_fusion.1
  57.3 16.9 %fusion = f32[256,4,256]{2,1,0:T(4,128)S(1)} fusion(bf16[256,128,256]{2,1,0:T(8,128)(2,1)} %param.9, bf16[256,4,256]{2,1,0:T(4,128)(2,1)S(1)} %gather_fusion.1, pred[256]{0:T(512)(128)(4,1)S(1)} %get-tuple-element.9), kind=kOutput, calls=%fused_computation.8 | convolution fusion | flops 134610944 | bytes 18350336 | tf_op jit(solution)/shard_map/bsc,bks->bkc/dot_general | solution.py:79
  74.1 1.4 broadcast_in_dim.38
  75.5 23.9 %scatter_fusion = f32[384,4,256]{2,1,0:T(4,128)} fusion(f32[384,4,256]{2,1,0:T(4,128)} %broadcast_in_dim.38, s32[256]{0:T(256)S(1)} %bitcast.49, f32[256,4,256]{2,1,0:T(4,128)S(1)} %fusion), kind=kCustom, calls=%fused_computation.3 | custom fusion | bytes 3146752 | tf_op jit(solution)/shard_map/scatter | solution.py:80
  99.4 4.3 %all-to-all-start.2 = ((f32[128,3,4,256]{3,2,1,0:T(4,128)}), f32[128,3,4,256]{3,2,1,0:T(4,128)S(1)}, u32[]{:S(2)}, u32[]{:S(2)}) async-start(f32[128,3,4,256]{3,2,1,0:T(4,128)} %bitcast.12), calls=%async_computation.2 | async-start | bytes 3145728 | tf_op jit(solution)/shard_map/all_to_all | solution.py:81
  103.7 3.1 %collective-permute-start.1 = (bf16[4,1,256]{2,1,0:T(2,128)(2,1)S(1)}, bf16[4,1,256]{2,1,0:T(2,128)(2,1)S(1)}, u32[]{:S(2)}, u32[]{:S(2)}) collective-permute-start(bf16[4,1,256]{2,1,0:T(2,128)(2,1)S(1)} %get-tuple-element.16), channel_id=1, source_target_pairs={{16,0},{32,16},{48,32},{64,48},{80,64},{96,80},{112,96},{17,1},{33... | collective-permute-start | bytes 6152 | tf_op jit(solution)/shard_map/ppermute | solution.py:20
  106.8 2.4 collective-permute-start
  109.3 13.3 %collective-permute-done.1 = bf16[4,1,256]{2,1,0:T(2,128)(2,1)S(1)} collective-permute-done((bf16[4,1,256]{2,1,0:T(2,128)(2,1)S(1)}, bf16[4,1,256]{2,1,0:T(2,128)(2,1)S(1)}, u32[]{:S(2)}, u32[]{:S(2)}) %collective-permute-start.1) | collective-permute-done | bytes 2080 | tf_op jit(solution)/shard_map/ppermute | solution.py:20
  122.7 1.5 collective-permute-start.3
  124.2 4.0 %collective-permute-start.2 = (bf16[4,130,1]{2,1,0:T(8,128)(2,1)S(1)}, bf16[4,130,1]{2,1,0:T(8,128)(2,1)S(1)}, u32[]{:S(2)}, u32[]{:S(2)}) collective-permute-start(bf16[4,130,1]{2,1,0:T(8,128)(2,1)S(1)} %get-tuple-element.13), channel_id=1, source_target_pairs={{0,1},{1,2},{2,3},{3,4},{4,5},{5,6},{6,7},{7,8},{8,9},{9,10},{10,1... | collective-permute-start | bytes 3128 | tf_op jit(solution)/shard_map/ppermute | solution.py:19
  128.8 1.4 collective-permute-done.2
  130.6 14.7 %scatter_fusion.1 = f32[128,4,256]{2,1,0:T(4,128)S(1)} fusion(f32[128,4,256]{2,1,0:T(4,128)S(1)} %broadcast_in_dim.36, s32[384]{0:T(512)S(1)} %reshape.126, f32[384,4,256]{2,1,0:T(4,128)S(1)} %bitcast.39), kind=kCustom, calls=%fused_computation.4 | custom fusion | flops 393216 | bytes 4720128 | tf_op jit(solution)/shard_map/scatter-add | solution.py:89
  145.4 2.6 reshape.90
  148.0 5.9 %copy.31 = f32[4,8,16,16,16]{4,3,2,1,0:T(8,128)} copy(f32[4,8,16,16,16]{4,2,3,1,0:T(8,128)} %bitcast.37) | data formatting | bytes 1048576 | tf_op jit(solution)/shard_map/transpose | solution.py:37
  153.9 3.6 %reshape.91 = f32[4,128,256]{2,1,0:T(8,128)S(1)} reshape(f32[4,8,16,16,16]{4,3,2,1,0:T(8,128)} %copy.31) | data formatting | bytes 1048576 | tf_op jit(solution)/shard_map/reshape | solution.py:38
  158.1 71.8 %all-reduce = (f32[4]{0:T(128)S(1)}, f32[4]{0:T(128)S(1)}) all-reduce(f32[4]{0:T(128)S(1)} %get-tuple-element.17, f32[4]{0:T(128)S(1)} %get-tuple-element.7), channel_id=1, replica_groups=mesh['tx'=8,'ty'=16] {'tx','ty'}, use_global_device_ids=true, to_apply=%region_1.2 | all-reduce | flops 8 | bytes 64 | tf_op jit(solution)/shard_map/psum | solution.py:91
  230.1 62.5 %psum.23 = f32[4]{0:T(128)S(1)} all-reduce(f32[4]{0:T(128)S(1)} %get-tuple-element.5), channel_id=1, replica_groups=mesh['tx'=8,'ty'=16] {'tx','ty'}, use_global_device_ids=true, to_apply=%region_11.12 | all-reduce | flops 4 | bytes 32 | tf_op jit(solution)/shard_map/psum | solution.py:95
  292.7 1.2 multiply_add_fusion
  (37 shorter events, 4.1 us)
Async XLA Ops:
  5.7 21.2 %all-to-all-start = ((s32[128,1,3]{2,1,0:T(1,128)}), s32[128,1,3]{2,1,0:T(1,128)S(1)}, u32[]{:S(2)}, u32[]{:S(2)}) async-start(s32[128,1,3]{2,1,0:T(1,128)} %bitcast.7), calls=%async_computation | async-start | bytes 131072 | tf_op jit(solution)/shard_map/all_to_all | solution.py:61
  31.4 24.7 %all-to-all-start.1 = ((bf16[128,3,4,256]{3,2,1,0:T(4,128)(2,1)}), bf16[128,3,4,256]{3,2,1,0:T(4,128)(2,1)S(1)}, u32[]{:S(2)}, u32[]{:S(2)}) async-start(bf16[128,3,4,256]{3,2,1,0:T(4,128)(2,1)} %broadcast_select_fusion), calls=%async_computation.1 | async-start | bytes 1572864 | tf_op jit(solution)/shard_map/all_to_all | solution.py:67
  99.4 31.1 %all-to-all-start.2 = ((f32[128,3,4,256]{3,2,1,0:T(4,128)}), f32[128,3,4,256]{3,2,1,0:T(4,128)S(1)}, u32[]{:S(2)}, u32[]{:S(2)}) async-start(f32[128,3,4,256]{3,2,1,0:T(4,128)} %bitcast.12), calls=%async_computation.2 | async-start | bytes 3145728 | tf_op jit(solution)/shard_map/all_to_all | solution.py:81
  103.7 18.9 %collective-permute-start.1 = (bf16[4,1,256]{2,1,0:T(2,128)(2,1)S(1)}, bf16[4,1,256]{2,1,0:T(2,128)(2,1)S(1)}, u32[]{:S(2)}, u32[]{:S(2)}) collective-permute-start(bf16[4,1,256]{2,1,0:T(2,128)(2,1)S(1)} %get-tuple-element.16), channel_id=1, source_target_pairs={{16,0},{32,16},{48,32},{64,48},{80,64},{96,80},{112,96},{17,1},{33... | collective-permute-start | bytes 6152 | tf_op jit(solution)/shard_map/ppermute | solution.py:20
  106.8 15.7 %collective-permute-start = (bf16[4,1,256]{2,1,0:T(2,128)(2,1)S(1)}, bf16[4,1,256]{2,1,0:T(2,128)(2,1)S(1)}, u32[]{:S(2)}, u32[]{:S(2)}) collective-permute-start(bf16[4,1,256]{2,1,0:T(2,128)(2,1)S(1)} %get-tuple-element.15), channel_id=1, source_target_pairs={{0,16},{16,32},{32,48},{48,64},{64,80},{80,96},{96,112},{1,17},{17... | collective-permute-start | bytes 6152 | tf_op jit(solution)/shard_map/ppermute | solution.py:19
  122.7 6.1 %collective-permute-start.3 = (bf16[4,130,1]{2,1,0:T(8,128)(2,1)S(1)}, bf16[4,130,1]{2,1,0:T(8,128)(2,1)S(1)}, u32[]{:S(2)}, u32[]{:S(2)}) collective-permute-start(bf16[4,130,1]{2,1,0:T(8,128)(2,1)S(1)} %get-tuple-element.14), channel_id=1, source_target_pairs={{1,0},{2,1},{3,2},{4,3},{5,4},{6,5},{7,6},{8,7},{9,8},{10,9},{11,1... | collective-permute-start | bytes 3128 | tf_op jit(solution)/shard_map/ppermute | solution.py:20
  124.2 6.0 %collective-permute-start.2 = (bf16[4,130,1]{2,1,0:T(8,128)(2,1)S(1)}, bf16[4,130,1]{2,1,0:T(8,128)(2,1)S(1)}, u32[]{:S(2)}, u32[]{:S(2)}) collective-permute-start(bf16[4,130,1]{2,1,0:T(8,128)(2,1)S(1)} %get-tuple-element.13), channel_id=1, source_target_pairs={{0,1},{1,2},{2,3},{3,4},{4,5},{5,6},{6,7},{7,8},{8,9},{9,10},{10,1... | collective-permute-start | bytes 3128 | tf_op jit(solution)/shard_map/ppermute | solution.py:19
  153.9 3.6 %copy-start = (f32[4,128,256]{2,1,0:T(8,128)S(1)}, f32[4,128,256]{2,1,0:T(8,128)}, u32[]{:S(2)}) copy-start(f32[4,128,256]{2,1,0:T(8,128)} %param.8) | copy-start | bytes 1572868
  153.9 3.6 %copy-start.1 = (f32[4,128,256]{2,1,0:T(8,128)S(1)}, f32[4,128,256]{2,1,0:T(8,128)}, u32[]{:S(2)}) copy-start(f32[4,128,256]{2,1,0:T(8,128)} %param.7) | copy-start | bytes 1572868
  157.5 135.1 %copy-start.3 = (f32[4,128,256]{2,1,0:T(8,128)S(1)}, f32[4,128,256]{2,1,0:T(8,128)}, u32[]{:S(2)}) copy-start(f32[4,128,256]{2,1,0:T(8,128)} %param.6) | copy-start | bytes 1572868
  230.1 63.7 %copy-start.2 = (f32[4,128,256]{2,1,0:T(8,128)}, f32[4,128,256]{2,1,0:T(8,128)S(1)}, u32[]{:S(2)}) copy-start(f32[4,128,256]{2,1,0:T(8,128)S(1)} %get-tuple-element.6) | copy-start | bytes 1572868
where the time goes:
time: 295 us; the launch traced here: 294 us
  blocking collectives  134 us (45%)
  local copies, waits for them, and re-layouts  51.6 us (17%)
  starting transfers between devices  34.8 us (12%)
  waiting for transfers between devices  33.7 us (11%)
  other arithmetic  21.7 us (7%)
  matrix products  16.9 us (6%)
    psum x1, blocking collectives, per_device(): norm_old = lax.psum(jnp.sum(residual * residual, axis=(1, 2)), ('tx', 'ty'))  71.8 us
    psum x1, blocking collectives, per_device(): lax.psum(jnp.sum(next_residual * next_residual, axis=(1, 2)), ('tx', 'ty'))  62.5 us
    scatter x1, local copies, waits for them, and re-layouts, per_device(): jnp.zeros((devices * cap, beacons, cells), jnp.float32).at[slot]  23.9 us
    dot_general x1, matrix products, per_device(): jnp.einsum('bsc,bks->bkc', blocks, samples, preferred_element_type=jnp.fl...  16.9 us
    all_to_all x1, waiting for transfers between devices, per_device(): lax.all_to_all(outgoing.reshape(devices, cap, beacons, cells), ('tx', 'ty...  16.6 us
    scatter-add x1, other arithmetic, per_device(): data_tiles = jnp.zeros(own_tiles.shape, jnp.float32).at[wanted].add(arrived)  14.7 us
    ppermute x2, waiting for transfers between devices, padded_2(): after = lax.ppermute(initial, axis, down)  13.9 us
    all_to_all x1, starting transfers between devices, per_device(): lax.all_to_all(request.reshape(devices, cap), ('tx', 'ty'), split_axis=0,...  11.5 us
  transfers between devices with their start and end apart: 7, of which 5 were waited for; matrix products, arithmetic and copies ran while one was open for 3% of the time, Pallas kernels for 0%

commit v1 on v0

v1 whole, which is shorter than its diff:
```python
import functools

import jax
import jax.numpy as jnp
from jax import lax
from jax.experimental import pallas as pl
from jax.experimental.pallas import tpu as pltpu
from jax.sharding import PartitionSpec as P

SIDE = 16
CAP = 3
GROUP = 8
SMOOTH = 0.25
MESH = pl.DeviceIdType.MESH
F32 = jnp.float32
BF16 = jnp.bfloat16
NT = (((1,), (1,)), ((), ()))
NN = (((1,), (0,)), ((), ()))


def swap_blocks(regs, lane):
    for j in (4, 2, 1):
        low = ((lane >> 4) & j) == 0
        made = list(regs)
        for r in range(8):
            if r & j == 0:
                a, b = regs[r], regs[r + j]
                made[r] = jnp.where(low, a, pltpu.roll(b, 16 * j, 1))
                made[r + j] = jnp.where(low, pltpu.roll(a, 128 - 16 * j, 1), b)
        regs = made
    return regs


def fold(x):
    rows, cols = x.shape
    y = x.reshape(rows // 8, 8, cols).sum(axis=0)
    return sum(y[:, c : c + 128] for c in range(0, cols, 128))


def fold_max(x):
    rows, cols = x.shape
    y = x.reshape(rows // 8, 8, cols).max(axis=0)
    out = y[:, :128]
    for c in range(128, cols, 128):
        out = jnp.maximum(out, y[:, c : c + 128])
    return out


def kernel(
    nx,
    ny,
    owner_ref,
    tile_ref,
    dir_ref,
    res_ref,
    blocks_ref,
    image_ref,
    coef_ref,
    bl,
    t1,
    t2,
    own,
    sb,
    fetched,
    ret,
    arrived,
    acc_ref,
    fld,
    til,
    hr,
    hrin,
    hc,
    hcin,
    bins_v,
    want_v,
    s1,
    s2,
    bins_s,
    want_s,
    sem_bl,
    sem_loc,
    sem_req,
    sem_halo,
    sem_dir,
    sem_ret,
    sem_send,
    sem_red,
):
    n = nx * ny
    beacons, rows, cols = dir_ref.shape
    count = owner_ref.shape[1]
    groups = n // GROUP
    tx, ty = lax.axis_index("tx"), lax.axis_index("ty")

    def ahead(k):
        return lax.rem(tx + k // ny, nx), lax.rem(ty + k % ny, ny)

    def behind(k):
        return lax.rem(tx + nx - k // ny, nx), lax.rem(ty + ny - k % ny, ny)

    def send(src, dst, send_sem, recv_sem, device):
        pltpu.make_async_remote_copy(
            src_ref=src,
            dst_ref=dst,
            send_sem=send_sem,
            recv_sem=recv_sem,
            device_id=device,
            device_id_type=MESH,
        ).start()

    def drain(ref, sem):
        pltpu.make_async_copy(ref, ref, sem).wait()

    blocks_copy = pltpu.make_async_copy(blocks_ref, bl, sem_bl)
    blocks_copy.start()

    barrier = pltpu.get_barrier_semaphore()
    for a in range(1, nx):
        pl.semaphore_signal(barrier, inc=1, device_id=(lax.rem(tx + a, nx), ty), device_id_type=MESH)
    for b in range(1, ny):
        pl.semaphore_signal(barrier, inc=1, device_id=(tx, lax.rem(ty + b, ny)), device_id_type=MESH)

    lane = lax.broadcasted_iota(jnp.int32, (8, 128), 1)
    row = lax.broadcasted_iota(jnp.int32, (8, 128), 0)

    with jax.named_scope("requests"):
        owner = owner_ref[...]
        ox, oy = owner // ny, lax.rem(owner, ny)
        dx, dy = ox - tx, oy - ty
        rel = jnp.where(dx < 0, dx + nx, dx) * ny + jnp.where(dy < 0, dy + ny, dy)
        member = rel == lax.broadcasted_iota(jnp.int32, (128, count), 0)
        earlier = lax.broadcasted_iota(jnp.int32, (count, count), 0) < lax.broadcasted_iota(
            jnp.int32, (count, count), 1
        )
        before = lax.dot_general(
            member.astype(F32).astype(BF16),
            earlier.astype(F32).astype(BF16),
            NN,
            preferred_element_type=F32,
        )
        told = lax.broadcasted_iota(jnp.int32, (16, count), 0)
        bin_no = lax.broadcasted_iota(jnp.int32, (16, count), 1)
        payload = jnp.where(told < 8, tile_ref[...] + 1, bin_no + 1).astype(F32)
        slots = jnp.zeros((16, 128), F32)
        for r in range(CAP):
            chosen = jnp.where(member, jnp.where(before == float(r), 1.0, 0.0), 0.0).astype(BF16)
            mine = jnp.where((told & 7) == r, payload, 0.0).astype(BF16)
            slots += lax.dot_general(mine, chosen, NT, preferred_element_type=F32)
        slots = slots - 1.0
        bins_v[...] = jnp.maximum(slots[8:], 0.0).astype(jnp.int32)
        bins_copy = pltpu.make_async_copy(bins_v, bins_s, sem_loc.at[0])
        bins_copy.start()

        table = jnp.where(row < CAP, slots[:8], 0.0)
        for b in range(beacons):
            norm = jnp.sum(fold(res_ref[b] * res_ref[b]), axis=0, keepdims=True)
            table = jnp.where(row == 4 + b, norm, table)
            high = jnp.max(fold_max(jnp.abs(dir_ref[b])), axis=0, keepdims=True)
            high = jnp.broadcast_to(high, (8, 128))
            high = jnp.maximum(high, pltpu.roll(high, 64, 1))
            high = jnp.maximum(high, pltpu.roll(high, 32, 1))
            table = jnp.where((row == 3) & ((lane >> 5) == b), high, table)
        t1[0] = table

    columns = jnp.zeros((rows, 128), F32)
    lane_r = lax.broadcasted_iota(jnp.int32, (rows, 128), 1)
    for b in range(beacons):
        hr[b : b + 1, :] = dir_ref[b, 0:1, :]
        hr[4 + b : 5 + b, :] = dir_ref[b, rows - 1 : rows, :]
        columns = jnp.where(lane_r == b, dir_ref[b, :, 0:1], columns)
        columns = jnp.where(lane_r == 4 + b, dir_ref[b, :, cols - 1 : cols], columns)
    hc[...] = columns.T[:8]

    pl.semaphore_wait(barrier, nx - 1 + ny - 1)

    for a in range(1, nx):
        send(t1.at[0], t1.at[a], sem_req.at[0], sem_req.at[1], (lax.rem(tx + a, nx), ty))
    send(hr, hrin.at[0], sem_halo.at[4], sem_halo.at[0], (lax.rem(tx + nx - 1, nx), ty))
    send(hr, hrin.at[1], sem_halo.at[5], sem_halo.at[1], (lax.rem(tx + 1, nx), ty))
    send(hc, hcin.at[0], sem_halo.at[6], sem_halo.at[2], (tx, lax.rem(ty + ny - 1, ny)))
    send(hc, hcin.at[1], sem_halo.at[7], sem_halo.at[3], (tx, lax.rem(ty + 1, ny)))

    with jax.named_scope("tiles"):
        for b in range(beacons):
            for s in range(rows // 8):
                at = (s // 2) * 64 + (s % 2) * 32 + b * 8
                for half in range(2):
                    fld[half, at : at + 8, :] = dir_ref[b, s * 8 : s * 8 + 8, half * 128 : half * 128 + 128]

        def cut(ti, carry):
            for half in range(2):
                regs = [fld[half, pl.ds(ti * 64 + r, 8, stride=8), :] for r in range(8)]
                for q, reg in enumerate(swap_blocks(regs, lane)):
                    own[ti * 16 + half * 8 + q] = reg.astype(BF16)
            return carry

        lax.fori_loop(0, rows // SIDE, cut, 0)

    def combine(tables, place, total):
        asked, high, summed = tables[0], tables[0], tables[0]
        for i in range(1, total):
            asked = jnp.where(place == i, tables[i], asked)
            high = jnp.maximum(high, tables[i])
            summed = summed + tables[i]
        return jnp.where(row < CAP, asked, jnp.where(row == CAP, high, summed))

    drain(t1.at[pl.ds(1, nx - 1)], sem_req.at[1])
    t2[0] = combine(t1, lane // ny, nx)
    for b in range(1, ny):
        send(t2.at[0], t2.at[b], sem_req.at[2], sem_req.at[3], (tx, lax.rem(ty + b, ny)))
    drain(t2.at[pl.ds(1, ny - 1)], sem_req.at[3])
    table = combine(t2, lax.rem(lane, ny), ny)
    want_v[...] = jnp.maximum(table, 0.0).astype(jnp.int32)
    want_copy = pltpu.make_async_copy(want_v, want_s, sem_loc.at[1])
    want_copy.start()
    want_copy.wait()

    with jax.named_scope("serve"):

        def serve(g, carry):
            for i in range(GROUP):
                k = g * GROUP + i
                for r in range(CAP):
                    sb[k, r] = own[jnp.clip(want_s[r, k], 0, own.shape[0] - 1)]

                def far():
                    send(sb.at[k], fetched.at[k], sem_send.at[0], sem_dir.at[g], behind(k))

                def near():
                    pltpu.make_async_copy(sb.at[k], fetched.at[k], sem_dir.at[g]).start()

                if i == 0:
                    pl.when(g == 0)(near)
                    pl.when(g > 0)(far)
                else:
                    far()
            return carry

        lax.fori_loop(0, groups, serve, 0)

    with jax.named_scope("laplace"):
        for i in range(2):
            drain(hrin.at[i], sem_halo.at[i])
            drain(hcin.at[i], sem_halo.at[2 + i])
        below = jnp.where(tx == nx - 1, 0.0, hrin[0])
        above = jnp.where(tx == 0, 0.0, hrin[1])
        right = jnp.where(ty == ny - 1, 0.0, hcin[0])
        left = jnp.where(ty == 0, 0.0, hcin[1])
        side = jnp.where(row < 4, right, left)
        side = jnp.concatenate([side, jnp.zeros((120, 128), F32)], axis=0).T
        row_f = lax.broadcasted_iota(jnp.int32, (rows, cols), 0)
        col_f = lax.broadcasted_iota(jnp.int32, (rows, cols), 1)
        for b in range(beacons):
            d = dir_ref[b]
            up = jnp.where(row_f == 0, above[4 + b : 5 + b], pltpu.roll(d, 1, 0))
            down = jnp.where(row_f == rows - 1, below[b : b + 1], pltpu.roll(d, rows - 1, 0))
            west = jnp.where(col_f == 0, side[:rows, 4 + b : 5 + b], pltpu.roll(d, 1, 1))
            east = jnp.where(col_f == cols - 1, side[:rows, b : b + 1], pltpu.roll(d, cols - 1, 1))
            image_ref[b] = SMOOTH * (4.0 * d - (down + up + east + west))

    bins_copy.wait()
    blocks_copy.wait()

    low = row < 4

    def products(g, carry):
        drain(fetched.at[pl.ds(g * GROUP, GROUP)], sem_dir.at[g])
        spots = [(g * GROUP + i // CAP, i % CAP) for i in range(GROUP * CAP)]
        ids = [jnp.clip(bins_s[r, k], 0, count - 1) for k, r in spots]
        parts = []
        for i in range(0, GROUP * CAP, 2):
            (kx, rx), (ky, ry) = spots[i : i + 2]
            x, y = fetched[kx, rx].astype(F32), fetched[ky, ry].astype(F32)
            first = jnp.where(low, x, pltpu.roll(y, 4, 0))
            second = jnp.where(low, pltpu.roll(x, 4, 0), y)
            parts.append(jnp.concatenate([first, second], axis=1))
        parts += [jnp.zeros((8, 256), F32)] * ((128 - 4 * GROUP * CAP) // 8)
        picked = jnp.concatenate(parts, axis=0).astype(BF16)
        held = None
        for i in range(GROUP * CAP):
            part = lax.dot_general(bl[ids[i]], picked, NT, preferred_element_type=F32).reshape(16, 8, 128)
            held = part if held is None else jnp.where(((lane >> 2) == i)[None], part, held)
        samples = held.reshape(128, 128).T.astype(BF16)
        for i in range(0, GROUP * CAP, 2):
            pair = samples[i * 4 : i * 4 + 8]
            x = lax.dot_general(pair, bl[ids[i]], NN, preferred_element_type=F32)
            y = lax.dot_general(pair, bl[ids[i + 1]], NN, preferred_element_type=F32)
            (kx, rx), (ky, ry) = spots[i : i + 2]
            ret[kx, rx] = jnp.where(low, x[:, :128], pltpu.roll(x[:, 128:], 4, 0)).astype(BF16)
            ret[ky, ry] = jnp.where(low, pltpu.roll(y[:, :128], 4, 0), y[:, 128:]).astype(BF16)
        for i in range(GROUP):
            k = g * GROUP + i

            def far():
                send(ret.at[k], arrived.at[k], sem_send.at[1], sem_ret.at[g], ahead(k))

            def near():
                pltpu.make_async_copy(ret.at[k], arrived.at[k], sem_ret.at[g]).start()

            if i == 0:
                pl.when(g == 0)(near)
                pl.when(g > 0)(far)
            else:
                far()
        return carry

    with jax.named_scope("products"):
        lax.fori_loop(0, groups, products, 0)

    with jax.named_scope("gather_up"):

        def widen(g, carry):
            drain(arrived.at[pl.ds(g * GROUP, GROUP)], sem_ret.at[g])
            for i in range(GROUP):
                for r in range(CAP):
                    at = pl.multiple_of((g * GROUP + i) * 8 * CAP + r * 8, 8)
                    acc_ref[pl.ds(at, 8), :] = arrived[g * GROUP + i, r].astype(F32)
            return carry

        lax.fori_loop(0, groups, widen, 0)

    with jax.named_scope("add_up"):
        number = lax.broadcasted_iota(jnp.int32, (128, n), 0).astype(F32)
        hits = jnp.concatenate(
            [jnp.where(number == table[r : r + 1, :n], 1.0, 0.0).astype(BF16) for r in range(CAP)], axis=1
        )
        for j in range(8):
            terms = jnp.concatenate(
                [acc_ref[pl.ds(r * 8 + j, n, stride=8 * CAP), :].astype(BF16) for r in range(CAP)], axis=0
            )
            til[pl.ds(j, 128, stride=8), :] = lax.dot_general(hits, terms, NN, preferred_element_type=F32)

        def paste(ti, carry):
            for half in range(2):
                regs = []
                for q in range(8):
                    at = pl.multiple_of((ti * 16 + half * 8 + q) * 8, 8)
                    regs.append(til[pl.ds(at, 8), :])
                for r, reg in enumerate(swap_blocks(regs, lane)):
                    fld[half, pl.ds(ti * 64 + r, 8, stride=8), :] = reg
            return carry

        lax.fori_loop(0, rows // SIDE, paste, 0)

    with jax.named_scope("sums"):
        first = jnp.zeros((8, 128), F32)
        second = jnp.zeros((8, 128), F32)
        scales = []
        for b in range(beacons):
            top = jnp.max(jnp.where((lane >> 5) == b, jnp.broadcast_to(table[3:4], (8, 128)), 0.0), axis=1, keepdims=True)
            top = jnp.maximum(jnp.broadcast_to(top, (8, 128)), 1e-30)
            scales.append(top)
            inverse = 1.0 / top
            dq = jnp.zeros((8, 128), F32)
            rq = jnp.zeros((8, 128), F32)
            qq = jnp.zeros((8, 128), F32)
            for s in range(rows // 8):
                at = (s // 2) * 64 + (s % 2) * 32 + b * 8
                for half in range(2):
                    span = (b, slice(s * 8, s * 8 + 8), slice(half * 128, half * 128 + 128))
                    q = fld[half, at : at + 8, :] + image_ref[span]
                    image_ref[span] = q
                    dq += dir_ref[span] * q
                    q = q * inverse
                    rq += res_ref[span] * q
                    qq += q * q
            dq = jnp.sum(dq, axis=0, keepdims=True)
            rq = jnp.sum(rq, axis=0, keepdims=True)
            qq = jnp.sum(qq, axis=0, keepdims=True)
            dq = jnp.broadcast_to(dq, (8, 128))
            rq = jnp.broadcast_to(rq, (8, 128))
            both = jnp.where(lane < 64, dq + pltpu.roll(dq, 64, 1), rq + pltpu.roll(rq, 64, 1))
            first = jnp.where(row == b, both, first)
            second = jnp.where(row == 4 + b, qq, second)
        s1[0] = jnp.where(row < 4, first, second)

    with jax.named_scope("reduce"):
        for b in range(1, ny):
            send(s1.at[0], s1.at[b], sem_red.at[0], sem_red.at[1], (tx, lax.rem(ty + b, ny)))
        drain(s1.at[pl.ds(1, ny - 1)], sem_red.at[1])
        total = s1[0]
        for b in range(1, ny):
            total = total + s1[b]
        s2[0] = total
        for a in range(1, nx):
            send(s2.at[0], s2.at[a], sem_red.at[2], sem_red.at[3], (lax.rem(tx + a, nx), ty))
        drain(s2.at[pl.ds(1, nx - 1)], sem_red.at[3])
        total = s2[0]
        for a in range(1, nx):
            total = total + s2[a]

        def whole(x):
            return jnp.broadcast_to(jnp.sum(x, axis=1, keepdims=True), (8, 128))

        norm_old = pltpu.roll(whole(table), 4, 0)
        curvature = whole(jnp.where(lane < 64, total, 0.0))
        cross = whole(jnp.where(lane < 64, 0.0, total))
        square = pltpu.roll(whole(total), 4, 0)
        top = scales[0]
        for b in range(1, beacons):
            top = jnp.where(row == b, scales[b], top)
        alpha = norm_old / curvature
        step = alpha * top
        norm_new = jnp.maximum(norm_old - 2.0 * step * cross + step * step * square, 0.0)
        beta = norm_new / norm_old
        coef_ref[...] = jnp.where(row < 4, alpha, pltpu.roll(beta, 4, 0))

    drain(t1.at[pl.ds(1, nx - 1)], sem_req.at[0])
    drain(t2.at[pl.ds(1, ny - 1)], sem_req.at[2])
    for i in range(2):
        drain(hr, sem_halo.at[4 + i])
        drain(hc, sem_halo.at[6 + i])
    drain(sb.at[pl.ds(1, n - 1)], sem_send.at[0])
    drain(ret.at[pl.ds(1, n - 1)], sem_send.at[1])
    drain(s1.at[pl.ds(1, ny - 1)], sem_red.at[0])
    drain(s2.at[pl.ds(1, nx - 1)], sem_red.at[2])


def per_device(nx, ny, solution, residual, direction, blocks, bin_owner, bin_tile):
    n = nx * ny
    beacons, rows, cols = direction.shape
    count = blocks.shape[0]
    vmem = pl.BlockSpec(memory_space=pltpu.VMEM)
    groups = n // GROUP
    slots = (n, CAP, 8, 128)
    image, coef = pl.pallas_call(
        functools.partial(kernel, nx, ny),
        out_shape=(
            jax.ShapeDtypeStruct(direction.shape, F32),
            jax.ShapeDtypeStruct((8, 128), F32),
        ),
        in_specs=[vmem] * 4 + [pl.BlockSpec(memory_space=pl.ANY)],
        out_specs=(vmem, vmem),
        scratch_shapes=[
            pltpu.VMEM(blocks.shape, BF16),
            pltpu.VMEM((nx, 8, 128), F32),
            pltpu.VMEM((ny, 8, 128), F32),
            pltpu.VMEM((128, 8, 128), BF16),
            pltpu.VMEM(slots, BF16),
            pltpu.VMEM(slots, BF16),
            pltpu.VMEM(slots, BF16),
            pltpu.VMEM(slots, BF16),
            pltpu.VMEM(((n + 1) * CAP * 8, 128), F32),
            pltpu.VMEM((2, beacons * rows + 8, 128), F32),
            pltpu.VMEM((1032, 128), F32),
            pltpu.VMEM((8, cols), F32),
            pltpu.VMEM((2, 8, cols), F32),
            pltpu.VMEM((8, 128), F32),
            pltpu.VMEM((2, 8, 128), F32),
            pltpu.VMEM((8, 128), jnp.int32),
            pltpu.VMEM((8, 128), jnp.int32),
            pltpu.VMEM((ny, 8, 128), F32),
            pltpu.VMEM((nx, 8, 128), F32),
            pltpu.SMEM((8, 128), jnp.int32),
            pltpu.SMEM((8, 128), jnp.int32),
            pltpu.SemaphoreType.DMA,
            pltpu.SemaphoreType.DMA((2,)),
            pltpu.SemaphoreType.DMA((4,)),
            pltpu.SemaphoreType.DMA((8,)),
            pltpu.SemaphoreType.DMA((groups,)),
            pltpu.SemaphoreType.DMA((groups,)),
            pltpu.SemaphoreType.DMA((2,)),
            pltpu.SemaphoreType.DMA((4,)),
        ],
        compiler_params=pltpu.CompilerParams(
            collective_id=0, has_side_effects=True, vmem_limit_bytes=48 * 2**20
        ),
        cost_estimate=pl.CostEstimate(
            flops=4 * count * 128 * 256 * 4, bytes_accessed=blocks.size * 2, transcendentals=0
        ),
        name="radio_map",
    )(bin_owner.reshape(1, count), bin_tile.reshape(1, count), direction, residual, blocks)
    alpha = coef[:4, 0][:, None, None]
    beta = coef[4:, 0][:, None, None]
    next_residual = residual - alpha * image
    next_solution = solution + alpha * direction
    next_direction = next_residual + beta * direction
    return next_solution, next_residual, next_direction


def solution(mesh):
    field = P(None, "tx", "ty")
    return jax.shard_map(
        functools.partial(per_device, mesh.shape["tx"], mesh.shape["ty"]),
        mesh=mesh,
        in_specs=(field, field, field, P(("tx", "ty"), None, None), P(("tx", "ty"), None), P(("tx", "ty"))),
        out_specs=(field, field, field),
        check_vma=False,
    )
```

time: 295 us -> 61.1 us (0.21)
  blocking collectives: 134 us -> 0 us
  Pallas kernels: 0 us -> 55.3 us
  local copies, waits for them, and re-layouts: 51.6 us -> 3.58 us
  starting transfers between devices: 34.8 us -> 0 us
  waiting for transfers between devices: 33.7 us -> 0 us
  other arithmetic: 21.7 us -> 1.34 us
  matrix products: 16.9 us -> 0 us
    psum x2 -> x0, blocking collectives: 134 us -> none  [the longest x1 71.8 us: per_device(): norm_old = lax.psum(jnp.sum(residual * residual, axis=(1, 2)), ('tx', 'ty'))]
    pallas_call x0 -> x1, Pallas kernels: none -> 55.3 us  [per_device(): pl.pallas_call(functools.partial(kernel, nx, ny), out_shape=(jax.ShapeDty...]
    scatter x2 -> x0, local copies, waits for them, and re-layouts: 25.4 us -> none  [the longest x1 23.9 us: per_device(): jnp.zeros((devices * cap, beacons, cells), jnp.float32).at[slot]]
    all_to_all x3 -> x0, starting transfers between devices: 23.8 us -> none  [the longest x1 11.5 us: per_device(): lax.all_to_all(request.reshape(devices, cap), ('tx', 'ty'), split_axis=0,...]
    all_to_all x3 -> x0, waiting for transfers between devices: 18.4 us -> none  [the longest x1 16.6 us: per_device(): lax.all_to_all(outgoing.reshape(devices, cap, beacons, cells), ('tx', 'ty...]
    dot_general x1 -> x0, matrix products: 16.9 us -> none  [per_device(): jnp.einsum('bsc,bks->bkc', blocks, samples, preferred_element_type=jnp.fl...]
    ppermute x4 -> x0, waiting for transfers between devices: 15.3 us -> none  [the longest x2 13.9 us: padded_2(): after = lax.ppermute(initial, axis, down)]
    scatter-add x1 -> x0, other arithmetic: 14.7 us -> none  [per_device(): data_tiles = jnp.zeros(own_tiles.shape, jnp.float32).at[wanted].add(arrived)]
  transfers between devices with their start and end apart: 7 -> 0, of which waited for: 5 -> 0; matrix products, arithmetic and copies ran while one was open for 3% -> 0% of each run, Pallas kernels for 0% -> 0%
where the time goes in v1:
time: 61.1 us; the launch traced here: 60.9 us
  Pallas kernels  55.3 us (91%)
  local copies, waits for them, and re-layouts  3.58 us (6%)
  other arithmetic  1.34 us (2%)
  between operations  0.66 us (1%)
    pallas_call x1, Pallas kernels, per_device(): pl.pallas_call(functools.partial(kernel, nx, ny), out_shape=(jax.ShapeDty...  55.3 us
    unnamed x10, local copies, waits for them, and re-layouts  3.44 us
    add x1, other arithmetic, per_device(): next_direction = next_residual + beta * direction  1.34 us

profile of v1, /device:TPU:1, one launch (start us, length us, event | category | flops | bytes accessed | tf_op | source)
XLA Modules:
  0.0 60.9 jit_solution(4279938062473032297)
XLA Ops:
  0.6 0.0 copy-start
  0.6 1.0 %copy-done = f32[4,128,256]{2,1,0:T(8,128)S(1)} copy-done((f32[4,128,256]{2,1,0:T(8,128)S(1)}, f32[4,128,256]{2,1,0:T(8,128)}, u32[]{:S(2)}) %copy-start) | copy-done | bytes 524312
  1.7 0.0 copy-start.1
  1.7 1.0 %copy-done.1 = f32[4,128,256]{2,1,0:T(8,128)S(1)} copy-done((f32[4,128,256]{2,1,0:T(8,128)S(1)}, f32[4,128,256]{2,1,0:T(8,128)}, u32[]{:S(2)}) %copy-start.1) | copy-done | bytes 524312
  2.7 0.0 copy-start.2
  2.7 0.7 %copy-done.2 = s32[256,1]{0,1:T(1,128)S(1)} copy-done((s32[256,1]{0,1:T(1,128)S(1)}, s32[256,1]{0,1:T(1,128)}, u32[]{:S(2)}) %copy-start.2) | copy-done | bytes 1048
  3.4 0.0 copy-start.3
  3.4 0.7 %copy-done.3 = s32[256]{0:T(256)S(1)} copy-done((s32[256]{0:T(256)S(1)}, s32[256]{0:T(256)}, u32[]{:S(2)}) %copy-start.3) | copy-done | bytes 1048
  4.1 0.0 copy-start.4
  4.1 55.3 %radio_map.1 = (f32[4,128,256]{2,1,0:T(8,128)S(1)}, f32[8,128]{1,0:T(8,128)S(1)}) custom-call(s32[1,256]{1,0:T(1,128)S(1)} %bitcast.2, s32[1,256]{1,0:T(1,128)S(1)} %bitcast.3, f32[4,128,256]{2,1,0:T(8,128)S(1)} %copy-done, f32[4,128,256]{2,1,0:T(8,128)S(1)} %copy-done.1, bf16[256,128,256]{2,1,0:T(8,128)(2,1)} %blocks_ref.1), custom_call_target="tpu_custom_call" | custom-call | flops 134217728 | bytes 16777216 | tf_op jit(solution)/shard_map/radio_map/pallas_call | solution.py:426
  59.4 0.1 slice_reduce_fusion
  59.5 0.0 copy-done.4
  59.5 1.3 %multiply_add_fusion = (f32[4,128,256]{2,1,0:T(8,128)}, f32[4,128,256]{2,1,0:T(8,128)}, f32[4,128,256]{2,1,0:T(8,128)}) fusion(f32[4,128,256]{2,1,0:T(8,128)S(1)} %copy-done, f32[4]{0:T(128)S(1)} %get-tuple-element.7, f32[4,128,256]{2,1,0:T(8,128)S(1)} %copy-done.1, f32[4,128,256]{2,1,0:T(8,128)S(1)} %get-tuple-element.6, f32[4]{0:T(128)S(1)} %get-tuple-element.8, ...), kind=kLoop, calls=%fused_computation | loop fusion | flops 786432 | bytes 3670048 | tf_op jit(solution)/shard_map/add | solution.py:477
Async XLA Ops:
  0.6 1.0 %copy-start = (f32[4,128,256]{2,1,0:T(8,128)S(1)}, f32[4,128,256]{2,1,0:T(8,128)}, u32[]{:S(2)}) copy-start(f32[4,128,256]{2,1,0:T(8,128)} %dir_ref.1) | copy-start | bytes 1572868
  1.7 1.0 %copy-start.1 = (f32[4,128,256]{2,1,0:T(8,128)S(1)}, f32[4,128,256]{2,1,0:T(8,128)}, u32[]{:S(2)}) copy-start(f32[4,128,256]{2,1,0:T(8,128)} %res_ref.1) | copy-start | bytes 1572868
  2.7 0.7 %copy-start.2 = (s32[256,1]{0,1:T(1,128)S(1)}, s32[256,1]{0,1:T(1,128)}, u32[]{:S(2)}) copy-start(s32[256,1]{0,1:T(1,128)} %param.10) | copy-start | bytes 3076
  3.4 0.7 %copy-start.3 = (s32[256]{0:T(256)S(1)}, s32[256]{0:T(256)}, u32[]{:S(2)}) copy-start(s32[256]{0:T(256)} %param.11) | copy-start | bytes 3076
  4.1 55.5 %copy-start.4 = (f32[4,128,256]{2,1,0:T(8,128)S(1)}, f32[4,128,256]{2,1,0:T(8,128)}, u32[]{:S(2)}) copy-start(f32[4,128,256]{2,1,0:T(8,128)} %param.6) | copy-start | bytes 1572868

commit v2 on v1

--- a/solution.py
+++ b/solution.py
@@ -49,13 +49,15 @@
 def kernel(
     nx,
     ny,
-    owner_ref,
-    tile_ref,
-    dir_ref,
-    res_ref,
+    bins_hbm,
+    dir_hbm,
+    res_hbm,
     blocks_ref,
     image_ref,
     coef_ref,
+    bins_ref,
+    dir_ref,
+    res_ref,
     bl,
     t1,
     t2,
@@ -74,7 +76,6 @@
     bins_v,
     want_v,
     s1,
-    s2,
     bins_s,
     want_s,
     sem_bl,
@@ -88,15 +89,24 @@
 ):
     n = nx * ny
     beacons, rows, cols = dir_ref.shape
-    count = owner_ref.shape[1]
+    count = bins_ref.shape[1]
     groups = n // GROUP
     tx, ty = lax.axis_index("tx"), lax.axis_index("ty")
 
-    def ahead(k):
-        return lax.rem(tx + k // ny, nx), lax.rem(ty + k % ny, ny)
-
-    def behind(k):
-        return lax.rem(tx + nx - k // ny, nx), lax.rem(ty + ny - k % ny, ny)
+    def place(g, i):
+        if ny % GROUP == 0:
+            return lax.div(g * GROUP, ny), lax.rem(g * GROUP, ny) + i
+        return lax.div(g * GROUP + i, ny), lax.rem(g * GROUP + i, ny)
+
+    def ahead(g, i):
+        a, b = place(g, i)
+        x, y = tx + a, ty + b
+        return jnp.where(x >= nx, x - nx, x), jnp.where(y >= ny, y - ny, y)
+
+    def behind(g, i):
+        a, b = place(g, i)
+        x, y = tx - a, ty - b
+        return jnp.where(x < 0, x + nx, x), jnp.where(y < 0, y + ny, y)
 
     def send(src, dst, send_sem, recv_sem, device):
         pltpu.make_async_remote_copy(
@@ -111,6 +121,14 @@
     def drain(ref, sem):
         pltpu.make_async_copy(ref, ref, sem).wait()
 
+    loads = [
+        pltpu.make_async_copy(src, dst, sem_loc.at[2 + i])
+        for i, (src, dst) in enumerate(
+            ((bins_hbm, bins_ref), (dir_hbm, dir_ref), (res_hbm, res_ref))
+        )
+    ]
+    for load in loads:
+        load.start()
     blocks_copy = pltpu.make_async_copy(blocks_ref, bl, sem_bl)
     blocks_copy.start()
 
@@ -124,7 +142,8 @@
     row = lax.broadcasted_iota(jnp.int32, (8, 128), 0)
 
     with jax.named_scope("requests"):
-        owner = owner_ref[...]
+        loads[0].wait()
+        owner, tile = bins_ref[...] >> 7, bins_ref[...] & 127
         ox, oy = owner // ny, lax.rem(owner, ny)
         dx, dy = ox - tx, oy - ty
         rel = jnp.where(dx < 0, dx + nx, dx) * ny + jnp.where(dy < 0, dy + ny, dy)
@@ -140,7 +159,7 @@
         )
         told = lax.broadcasted_iota(jnp.int32, (16, count), 0)
         bin_no = lax.broadcasted_iota(jnp.int32, (16, count), 1)
-        payload = jnp.where(told < 8, tile_ref[...] + 1, bin_no + 1).astype(F32)
+        payload = jnp.where(told < 8, tile + 1, bin_no + 1).astype(F32)
         slots = jnp.zeros((16, 128), F32)
         for r in range(CAP):
             chosen = jnp.where(member, jnp.where(before == float(r), 1.0, 0.0), 0.0).astype(BF16)
@@ -152,6 +171,8 @@
         bins_copy.start()
 
         table = jnp.where(row < CAP, slots[:8], 0.0)
+        loads[1].wait()
+        loads[2].wait()
         for b in range(beacons):
             norm = jnp.sum(fold(res_ref[b] * res_ref[b]), axis=0, keepdims=True)
             table = jnp.where(row == 4 + b, norm, table)
@@ -208,36 +229,6 @@
     t2[0] = combine(t1, lane // ny, nx)
     for b in range(1, ny):
         send(t2.at[0], t2.at[b], sem_req.at[2], sem_req.at[3], (tx, lax.rem(ty + b, ny)))
-    drain(t2.at[pl.ds(1, ny - 1)], sem_req.at[3])
-    table = combine(t2, lax.rem(lane, ny), ny)
-    want_v[...] = jnp.maximum(table, 0.0).astype(jnp.int32)
-    want_copy = pltpu.make_async_copy(want_v, want_s, sem_loc.at[1])
-    want_copy.start()
-    want_copy.wait()
-
-    with jax.named_scope("serve"):
-
-        def serve(g, carry):
-            for i in range(GROUP):
-                k = g * GROUP + i
-                for r in range(CAP):
-                    sb[k, r] = own[jnp.clip(want_s[r, k], 0, own.shape[0] - 1)]
-
-                def far():
-                    send(sb.at[k], fetched.at[k], sem_send.at[0], sem_dir.at[g], behind(k))
-
-                def near():
-                    pltpu.make_async_copy(sb.at[k], fetched.at[k], sem_dir.at[g]).start()
-
-                if i == 0:
-                    pl.when(g == 0)(near)
-                    pl.when(g > 0)(far)
-                else:
-                    far()
-            return carry
-
-        lax.fori_loop(0, groups, serve, 0)
-
     with jax.named_scope("laplace"):
         for i in range(2):
             drain(hrin.at[i], sem_halo.at[i])
@@ -258,6 +249,36 @@
             east = jnp.where(col_f == cols - 1, side[:rows, b : b + 1], pltpu.roll(d, cols - 1, 1))
             image_ref[b] = SMOOTH * (4.0 * d - (down + up + east + west))
 
+    drain(t2.at[pl.ds(1, ny - 1)], sem_req.at[3])
+    table = combine(t2, lax.rem(lane, ny), ny)
+    want_v[...] = jnp.maximum(table, 0.0).astype(jnp.int32)
+    want_copy = pltpu.make_async_copy(want_v, want_s, sem_loc.at[1])
+    want_copy.start()
+    want_copy.wait()
+
+    with jax.named_scope("serve"):
+
+        def serve(g, carry):
+            for i in range(GROUP):
+                k = g * GROUP + i
+                for r in range(CAP):
+                    sb[k, r] = own[jnp.clip(want_s[r, k], 0, own.shape[0] - 1)]
+
+                def far():
+                    send(sb.at[k], fetched.at[k], sem_send.at[0], sem_dir.at[g], behind(g, i))
+
+                def near():
+                    pltpu.make_async_copy(sb.at[k], fetched.at[k], sem_dir.at[g]).start()
+
+                if i == 0:
+                    pl.when(g == 0)(near)
+                    pl.when(g > 0)(far)
+                else:
+                    far()
+            return carry
+
+        lax.fori_loop(0, groups, serve, 0)
+
     bins_copy.wait()
     blocks_copy.wait()
 
@@ -267,22 +288,21 @@
         drain(fetched.at[pl.ds(g * GROUP, GROUP)], sem_dir.at[g])
         spots = [(g * GROUP + i // CAP, i % CAP) for i in range(GROUP * CAP)]
         ids = [jnp.clip(bins_s[r, k], 0, count - 1) for k, r in spots]
-        parts = []
+        picked = []
         for i in range(0, GROUP * CAP, 2):
             (kx, rx), (ky, ry) = spots[i : i + 2]
             x, y = fetched[kx, rx].astype(F32), fetched[ky, ry].astype(F32)
             first = jnp.where(low, x, pltpu.roll(y, 4, 0))
             second = jnp.where(low, pltpu.roll(x, 4, 0), y)
-            parts.append(jnp.concatenate([first, second], axis=1))
-        parts += [jnp.zeros((8, 256), F32)] * ((128 - 4 * GROUP * CAP) // 8)
-        picked = jnp.concatenate(parts, axis=0).astype(BF16)
-        held = None
-        for i in range(GROUP * CAP):
-            part = lax.dot_general(bl[ids[i]], picked, NT, preferred_element_type=F32).reshape(16, 8, 128)
-            held = part if held is None else jnp.where(((lane >> 2) == i)[None], part, held)
-        samples = held.reshape(128, 128).T.astype(BF16)
+            picked.append(jnp.concatenate([first, second], axis=1).astype(BF16))
+        pairs = []
         for i in range(0, GROUP * CAP, 2):
-            pair = samples[i * 4 : i * 4 + 8]
+            pair = picked[i // 2]
+            x = lax.dot_general(pair, bl[ids[i]], NT, preferred_element_type=F32)
+            y = lax.dot_general(pair, bl[ids[i + 1]], NT, preferred_element_type=F32)
+            pairs.append(jnp.where(low, x, y).astype(BF16))
+        for i in range(0, GROUP * CAP, 2):
+            pair = pairs[i // 2]
             x = lax.dot_general(pair, bl[ids[i]], NN, preferred_element_type=F32)
             y = lax.dot_general(pair, bl[ids[i + 1]], NN, preferred_element_type=F32)
             (kx, rx), (ky, ry) = spots[i : i + 2]
@@ -292,7 +312,7 @@
             k = g * GROUP + i
 
             def far():
-                send(ret.at[k], arrived.at[k], sem_send.at[1], sem_ret.at[g], ahead(k))
+                send(ret.at[k], arrived.at[k], sem_send.at[1], sem_ret.at[g], ahead(g, i))
 
             def near():
                 pltpu.make_async_copy(ret.at[k], arrived.at[k], sem_ret.at[g]).start()
@@ -307,7 +327,7 @@
     with jax.named_scope("products"):
         lax.fori_loop(0, groups, products, 0)
 
-    with jax.named_scope("gather_up"):
+    with jax.named_scope("add_up"):
 
         def widen(g, carry):
             drain(arrived.at[pl.ds(g * GROUP, GROUP)], sem_ret.at[g])
@@ -317,18 +337,22 @@
                     acc_ref[pl.ds(at, 8), :] = arrived[g * GROUP + i, r].astype(F32)
             return carry
 
-        lax.fori_loop(0, groups, widen, 0)
-
-    with jax.named_scope("add_up"):
-        number = lax.broadcasted_iota(jnp.int32, (128, n), 0).astype(F32)
-        hits = jnp.concatenate(
-            [jnp.where(number == table[r : r + 1, :n], 1.0, 0.0).astype(BF16) for r in range(CAP)], axis=1
-        )
-        for j in range(8):
-            terms = jnp.concatenate(
-                [acc_ref[pl.ds(r * 8 + j, n, stride=8 * CAP), :].astype(BF16) for r in range(CAP)], axis=0
+        number = lax.broadcasted_iota(jnp.int32, (128, 128), 0).astype(F32)
+        split = groups * 3 // 4
+        for start, stop in ((0, split), (split, groups)):
+            lax.fori_loop(start, stop, widen, 0)
+            k0, nk = start * GROUP, (stop - start) * GROUP
+            hits = jnp.concatenate(
+                [jnp.where(number == table[r : r + 1], 1.0, 0.0).astype(BF16)[:, k0 : k0 + nk] for r in range(CAP)],
+                axis=1,
             )
-            til[pl.ds(j, 128, stride=8), :] = lax.dot_general(hits, terms, NN, preferred_element_type=F32)
+            for j in range(8):
+                terms = [acc_ref[pl.ds((k0 * CAP + r) * 8 + j, nk, stride=8 * CAP), :] for r in range(CAP)]
+                terms = jnp.concatenate(terms, axis=0).astype(BF16)
+                part = lax.dot_general(hits, terms, NN, preferred_element_type=F32)
+                if start:
+                    part += til[pl.ds(j, 128, stride=8), :]
+                til[pl.ds(j, 128, stride=8), :] = part
 
         def paste(ti, carry):
             for half in range(2):
@@ -343,8 +367,9 @@
         lax.fori_loop(0, rows // SIDE, paste, 0)
 
     with jax.named_scope("sums"):
-        first = jnp.zeros((8, 128), F32)
-        second = jnp.zeros((8, 128), F32)
+        stack = jnp.zeros((16, 128), F32)
+        which = lax.broadcasted_iota(jnp.int32, (16, 128), 0)
+        spot = lax.broadcasted_iota(jnp.int32, (16, 128), 1) >> 3
         scales = []
         for b in range(beacons):
             top = jnp.max(jnp.where((lane >> 5) == b, jnp.broadcast_to(table[3:4], (8, 128)), 0.0), axis=1, keepdims=True)
@@ -364,38 +389,40 @@
                     q = q * inverse
                     rq += res_ref[span] * q
                     qq += q * q
-            dq = jnp.sum(dq, axis=0, keepdims=True)
-            rq = jnp.sum(rq, axis=0, keepdims=True)
-            qq = jnp.sum(qq, axis=0, keepdims=True)
-            dq = jnp.broadcast_to(dq, (8, 128))
-            rq = jnp.broadcast_to(rq, (8, 128))
-            both = jnp.where(lane < 64, dq + pltpu.roll(dq, 64, 1), rq + pltpu.roll(rq, 64, 1))
-            first = jnp.where(row == b, both, first)
-            second = jnp.where(row == 4 + b, qq, second)
-        s1[0] = jnp.where(row < 4, first, second)
+            for i, x in enumerate((dq, rq, qq)):
+                stack = jnp.where(which == 4 * i + b, jnp.sum(x, axis=0, keepdims=True), stack)
+        for shift in (64, 32, 16, 8):
+            stack = stack + pltpu.roll(stack, shift, 1)
+        s1[0:1, :] = jnp.sum(jnp.where(which == spot, stack, 0.0), axis=0, keepdims=True)
 
     with jax.named_scope("reduce"):
-        for b in range(1, ny):
-            send(s1.at[0], s1.at[b], sem_red.at[0], sem_red.at[1], (tx, lax.rem(ty + b, ny)))
-        drain(s1.at[pl.ds(1, ny - 1)], sem_red.at[1])
-        total = s1[0]
-        for b in range(1, ny):
-            total = total + s1[b]
-        s2[0] = total
-        for a in range(1, nx):
-            send(s2.at[0], s2.at[a], sem_red.at[2], sem_red.at[3], (lax.rem(tx + a, nx), ty))
-        drain(s2.at[pl.ds(1, nx - 1)], sem_red.at[3])
-        total = s2[0]
-        for a in range(1, nx):
-            total = total + s2[a]
+
+        def spread(g, carry):
+            for i in range(GROUP):
+
+                def far():
+                    k = g * GROUP + i
+                    send(s1.at[pl.ds(0, 1)], s1.at[pl.ds(k, 1)], sem_red.at[0], sem_red.at[1], ahead(g, i))
+
+                if i == 0:
+                    pl.when(g > 0)(far)
+                else:
+                    far()
+            return carry
+
+        lax.fori_loop(0, groups, spread, 0)
+        drain(s1.at[pl.ds(1, n - 1)], sem_red.at[1])
+        total = jnp.sum(s1[...], axis=0, keepdims=True)
+        total = jnp.sum(jnp.where(which == spot, total, 0.0), axis=1, keepdims=True)
+        total = jnp.broadcast_to(total, (16, 128))
 
         def whole(x):
             return jnp.broadcast_to(jnp.sum(x, axis=1, keepdims=True), (8, 128))
 
         norm_old = pltpu.roll(whole(table), 4, 0)
-        curvature = whole(jnp.where(lane < 64, total, 0.0))
-        cross = whole(jnp.where(lane < 64, 0.0, total))
-        square = pltpu.roll(whole(total), 4, 0)
+        curvature = total[:8]
+        cross = pltpu.roll(total[:8], 4, 0)
+        square = total[8:]
         top = scales[0]
         for b in range(1, beacons):
             top = jnp.where(row == b, scales[b], top)
@@ -412,8 +439,7 @@
         drain(hc, sem_halo.at[6 + i])
     drain(sb.at[pl.ds(1, n - 1)], sem_send.at[0])
     drain(ret.at[pl.ds(1, n - 1)], sem_send.at[1])
-    drain(s1.at[pl.ds(1, ny - 1)], sem_red.at[0])
-    drain(s2.at[pl.ds(1, nx - 1)], sem_red.at[2])
+    drain(s1.at[pl.ds(1, n - 1)], sem_red.at[0])
 
 
 def per_device(nx, ny, solution, residual, direction, blocks, bin_owner, bin_tile):
@@ -429,9 +455,12 @@
             jax.ShapeDtypeStruct(direction.shape, F32),
             jax.ShapeDtypeStruct((8, 128), F32),
         ),
-        in_specs=[vmem] * 4 + [pl.BlockSpec(memory_space=pl.ANY)],
+        in_specs=[pl.BlockSpec(memory_space=pl.ANY)] * 4,
         out_specs=(vmem, vmem),
         scratch_shapes=[
+            pltpu.VMEM((1, count), jnp.int32),
+            pltpu.VMEM(direction.shape, F32),
+            pltpu.VMEM(direction.shape, F32),
             pltpu.VMEM(blocks.shape, BF16),
             pltpu.VMEM((nx, 8, 128), F32),
             pltpu.VMEM((ny, 8, 128), F32),
@@ -449,27 +478,26 @@
             pltpu.VMEM((2, 8, 128), F32),
             pltpu.VMEM((8, 128), jnp.int32),
             pltpu.VMEM((8, 128), jnp.int32),
-            pltpu.VMEM((ny, 8, 128), F32),
-            pltpu.VMEM((nx, 8, 128), F32),
+            pltpu.VMEM((n, 128), F32),
             pltpu.SMEM((8, 128), jnp.int32),
             pltpu.SMEM((8, 128), jnp.int32),
             pltpu.SemaphoreType.DMA,
-            pltpu.SemaphoreType.DMA((2,)),
+            pltpu.SemaphoreType.DMA((5,)),
             pltpu.SemaphoreType.DMA((4,)),
             pltpu.SemaphoreType.DMA((8,)),
             pltpu.SemaphoreType.DMA((groups,)),
             pltpu.SemaphoreType.DMA((groups,)),
             pltpu.SemaphoreType.DMA((2,)),
-            pltpu.SemaphoreType.DMA((4,)),
+            pltpu.SemaphoreType.DMA((2,)),
         ],
         compiler_params=pltpu.CompilerParams(
-            collective_id=0, has_side_effects=True, vmem_limit_bytes=48 * 2**20
+            collective_id=0, has_side_effects=True, vmem_limit_bytes=53 * 2**20
         ),
         cost_estimate=pl.CostEstimate(
             flops=4 * count * 128 * 256 * 4, bytes_accessed=blocks.size * 2, transcendentals=0
         ),
         name="radio_map",
-    )(bin_owner.reshape(1, count), bin_tile.reshape(1, count), direction, residual, blocks)
+    )(bin_owner.reshape(1, count) * 128 + bin_tile.reshape(1, count), direction, residual, blocks)
     alpha = coef[:4, 0][:, None, None]
     beta = coef[4:, 0][:, None, None]
     next_residual = residual - alpha * image

time: 61.1 us -> 56.3 us (0.921)
  local copies, waits for them, and re-layouts: 3.58 us -> 0.16 us
  Pallas kernels: 55.3 us -> 52.5 us
  other arithmetic: 1.34 us -> 2.8 us
    unnamed x10 -> x6, local copies, waits for them, and re-layouts: 3.44 us -> 0.02 us
    pallas_call x1, Pallas kernels: 55.3 us -> 52.5 us  [per_device(): pl.pallas_call(functools.partial(kernel, nx, ny), out_shape=(jax.ShapeDty...]
    mul x0 -> x1, other arithmetic: none -> 0.8 us  [per_device(): bin_owner.reshape(1, count) * 128 + bin_tile.reshape(1, count)]
    add x0 -> x1, other arithmetic: none -> 0.68 us  [per_device(): bin_owner.reshape(1, count) * 128 + bin_tile.reshape(1, count)]
where the time goes in v2:
time: 56.3 us; the launch traced here: 56.1 us
  Pallas kernels  52.5 us (93%)
  other arithmetic  2.8 us (5%)
  between operations  0.69 us (1%)
    pallas_call x1, Pallas kernels, per_device(): pl.pallas_call(functools.partial(kernel, nx, ny), out_shape=(jax.ShapeDty...  52.5 us
    add x1, other arithmetic, per_device(): next_direction = next_residual + beta * direction  1.33 us

profile of v2, /device:TPU:1, one launch (start us, length us, event | category | flops | bytes accessed | tf_op | source)
XLA Modules:
  0.0 56.1 jit_solution(11860613374068907373)
XLA Ops:
  0.6 0.0 copy-start
  0.6 0.0 copy-start.1
  0.7 0.0 copy-start.2
  0.7 0.8 %broadcast_multiply_fusion = s32[256,1]{0,1:T(1,128)S(1)} fusion(s32[256,1]{0,1:T(1,128)} %param.10), kind=kLoop, calls=%fused_computation.5 | loop fusion | flops 256 | bytes 2048 | tf_op jit(solution)/shard_map/mul | solution.py:500
  1.5 0.7 %add.11 = s32[256]{0:T(256)S(1)} add(s32[256]{0:T(256)S(1)} %bitcast.3, s32[256]{0:T(256)} %param.11) | non-fusion elementwise | flops 256 | bytes 3072 | tf_op jit(solution)/shard_map/add | solution.py:500
  2.1 52.5 %radio_map.1 = (f32[4,128,256]{2,1,0:T(8,128)S(1)}, f32[8,128]{1,0:T(8,128)S(1)}) custom-call(s32[1,256]{1,0:T(1,128)S(1)} %bitcast.2, f32[4,128,256]{2,1,0:T(8,128)} %dir_hbm.1, f32[4,128,256]{2,1,0:T(8,128)} %res_hbm.1, bf16[256,128,256]{2,1,0:T(8,128)(2,1)} %blocks_ref.1), custom_call_target="tpu_custom_call" | custom-call | flops 134217728 | bytes 16777216 | tf_op jit(solution)/shard_map/radio_map/pallas_call | solution.py:452
  54.6 0.1 slice_reduce_fusion
  54.8 0.0 copy-done
  54.8 0.0 copy-done.1
  54.8 0.0 copy-done.2
  54.8 1.3 %multiply_add_fusion = (f32[4,128,256]{2,1,0:T(8,128)}, f32[4,128,256]{2,1,0:T(8,128)}, f32[4,128,256]{2,1,0:T(8,128)}) fusion(f32[4,128,256]{2,1,0:T(8,128)S(1)} %copy-done, f32[4]{0:T(128)S(1)} %get-tuple-element.7, f32[4,128,256]{2,1,0:T(8,128)S(1)} %copy-done.1, f32[4,128,256]{2,1,0:T(8,128)S(1)} %get-tuple-element.6, f32[4]{0:T(128)S(1)} %get-tuple-element.8, ...), kind=kLoop, calls=%fused_computation | loop fusion | flops 786432 | bytes 3670048 | tf_op jit(solution)/shard_map/add | solution.py:505
Async XLA Ops:
  0.6 54.2 %copy-start = (f32[4,128,256]{2,1,0:T(8,128)S(1)}, f32[4,128,256]{2,1,0:T(8,128)}, u32[]{:S(2)}) copy-start(f32[4,128,256]{2,1,0:T(8,128)} %dir_hbm.1) | copy-start | bytes 1572868
  0.6 54.2 %copy-start.1 = (f32[4,128,256]{2,1,0:T(8,128)S(1)}, f32[4,128,256]{2,1,0:T(8,128)}, u32[]{:S(2)}) copy-start(f32[4,128,256]{2,1,0:T(8,128)} %res_hbm.1) | copy-start | bytes 1572868
  0.7 54.1 %copy-start.2 = (f32[4,128,256]{2,1,0:T(8,128)S(1)}, f32[4,128,256]{2,1,0:T(8,128)}, u32[]{:S(2)}) copy-start(f32[4,128,256]{2,1,0:T(8,128)} %param.6) | copy-start | bytes 1572868

commit v3 on v2

--- a/solution.py
+++ b/solution.py
@@ -49,13 +49,15 @@
 def kernel(
     nx,
     ny,
-    bins_hbm,
+    owner_hbm,
+    tile_hbm,
     dir_hbm,
     res_hbm,
     blocks_ref,
     image_ref,
     coef_ref,
-    bins_ref,
+    owner_ref,
+    tile_ref,
     dir_ref,
     res_ref,
     bl,
@@ -89,7 +91,7 @@
 ):
     n = nx * ny
     beacons, rows, cols = dir_ref.shape
-    count = bins_ref.shape[1]
+    count = owner_ref.shape[1]
     groups = n // GROUP
     tx, ty = lax.axis_index("tx"), lax.axis_index("ty")
 
@@ -124,7 +126,7 @@
     loads = [
         pltpu.make_async_copy(src, dst, sem_loc.at[2 + i])
         for i, (src, dst) in enumerate(
-            ((bins_hbm, bins_ref), (dir_hbm, dir_ref), (res_hbm, res_ref))
+            ((owner_hbm, owner_ref), (tile_hbm, tile_ref), (dir_hbm, dir_ref), (res_hbm, res_ref))
         )
     ]
     for load in loads:
@@ -143,7 +145,8 @@
 
     with jax.named_scope("requests"):
         loads[0].wait()
-        owner, tile = bins_ref[...] >> 7, bins_ref[...] & 127
+        loads[1].wait()
+        owner, tile = owner_ref[...], tile_ref[...]
         ox, oy = owner // ny, lax.rem(owner, ny)
         dx, dy = ox - tx, oy - ty
         rel = jnp.where(dx < 0, dx + nx, dx) * ny + jnp.where(dy < 0, dy + ny, dy)
@@ -171,8 +174,8 @@
         bins_copy.start()
 
         table = jnp.where(row < CAP, slots[:8], 0.0)
-        loads[1].wait()
         loads[2].wait()
+        loads[3].wait()
         for b in range(beacons):
             norm = jnp.sum(fold(res_ref[b] * res_ref[b]), axis=0, keepdims=True)
             table = jnp.where(row == 4 + b, norm, table)
@@ -183,6 +186,11 @@
             table = jnp.where((row == 3) & ((lane >> 5) == b), high, table)
         t1[0] = table
 
+    pl.semaphore_wait(barrier, nx - 1 + ny - 1)
+
+    for a in range(1, nx):
+        send(t1.at[0], t1.at[a], sem_req.at[0], sem_req.at[1], (lax.rem(tx + a, nx), ty))
+
     columns = jnp.zeros((rows, 128), F32)
     lane_r = lax.broadcasted_iota(jnp.int32, (rows, 128), 1)
     for b in range(beacons):
@@ -191,11 +199,6 @@
         columns = jnp.where(lane_r == b, dir_ref[b, :, 0:1], columns)
         columns = jnp.where(lane_r == 4 + b, dir_ref[b, :, cols - 1 : cols], columns)
     hc[...] = columns.T[:8]
-
-    pl.semaphore_wait(barrier, nx - 1 + ny - 1)
-
-    for a in range(1, nx):
-        send(t1.at[0], t1.at[a], sem_req.at[0], sem_req.at[1], (lax.rem(tx + a, nx), ty))
     send(hr, hrin.at[0], sem_halo.at[4], sem_halo.at[0], (lax.rem(tx + nx - 1, nx), ty))
     send(hr, hrin.at[1], sem_halo.at[5], sem_halo.at[1], (lax.rem(tx + 1, nx), ty))
     send(hc, hcin.at[0], sem_halo.at[6], sem_halo.at[2], (tx, lax.rem(ty + ny - 1, ny)))
@@ -455,9 +458,10 @@
             jax.ShapeDtypeStruct(direction.shape, F32),
             jax.ShapeDtypeStruct((8, 128), F32),
         ),
-        in_specs=[pl.BlockSpec(memory_space=pl.ANY)] * 4,
+        in_specs=[pl.BlockSpec(memory_space=pl.ANY)] * 5,
         out_specs=(vmem, vmem),
         scratch_shapes=[
+            pltpu.VMEM((1, count), jnp.int32),
             pltpu.VMEM((1, count), jnp.int32),
             pltpu.VMEM(direction.shape, F32),
             pltpu.VMEM(direction.shape, F32),
@@ -482,7 +486,7 @@
             pltpu.SMEM((8, 128), jnp.int32),
             pltpu.SMEM((8, 128), jnp.int32),
             pltpu.SemaphoreType.DMA,
-            pltpu.SemaphoreType.DMA((5,)),
+            pltpu.SemaphoreType.DMA((6,)),
             pltpu.SemaphoreType.DMA((4,)),
             pltpu.SemaphoreType.DMA((8,)),
             pltpu.SemaphoreType.DMA((groups,)),
@@ -497,7 +501,13 @@
             flops=4 * count * 128 * 256 * 4, bytes_accessed=blocks.size * 2, transcendentals=0
         ),
         name="radio_map",
-    )(bin_owner.reshape(1, count) * 128 + bin_tile.reshape(1, count), direction, residual, blocks)
+    )(
+        pltpu.with_memory_space_constraint(bin_owner.reshape(1, count), pltpu.HBM),
+        pltpu.with_memory_space_constraint(bin_tile.reshape(1, count), pltpu.HBM),
+        direction,
+        residual,
+        blocks,
+    )
     alpha = coef[:4, 0][:, None, None]
     beta = coef[4:, 0][:, None, None]
     next_residual = residual - alpha * image

time: 56.3 us -> 54.9 us (0.975)
  other arithmetic: 2.8 us -> 1.31 us
    mul x1 -> x0, other arithmetic: 0.8 us -> none  [per_device(): bin_owner.reshape(1, count) * 128 + bin_tile.reshape(1, count)]
    add x1 -> x0, other arithmetic: 0.68 us -> none  [per_device(): bin_owner.reshape(1, count) * 128 + bin_tile.reshape(1, count)]
where the time goes in v3:
time: 54.9 us; the launch traced here: 54.8 us
  Pallas kernels  52.7 us (96%)
  other arithmetic  1.31 us (2%)
  between operations  0.69 us (1%)
    pallas_call x1, Pallas kernels, per_device(): pl.pallas_call(functools.partial(kernel, nx, ny), out_shape=(jax.ShapeDty...  52.7 us
    add x1, other arithmetic, per_device(): next_direction = next_residual + beta * direction  1.31 us

profile of v3, /device:TPU:1, one launch (start us, length us, event | category | flops | bytes accessed | tf_op | source)
XLA Modules:
  0.0 54.8 jit_solution(12950282055125684087)
XLA Ops:
  0.6 0.0 copy-start
  0.6 0.0 copy-start.1
  0.7 0.0 copy-start.2
  0.7 52.7 %radio_map.1 = (f32[4,128,256]{2,1,0:T(8,128)S(1)}, f32[8,128]{1,0:T(8,128)S(1)}) custom-call(s32[1,256]{1,0:T(1,128)} %bitcast.2, s32[1,256]{1,0:T(1,128)} %bitcast.3, f32[4,128,256]{2,1,0:T(8,128)} %dir_hbm.1, f32[4,128,256]{2,1,0:T(8,128)} %res_hbm.1, bf16[256,128,256]{2,1,0:T(8,128)(2,1)} %blocks_ref.1), custom_call_target="tpu_custom_call" | custom-call | flops 134217728 | bytes 16777216 | tf_op jit(solution)/shard_map/radio_map/pallas_call | solution.py:455
  53.3 0.1 slice_reduce_fusion
  53.5 0.0 copy-done
  53.5 0.0 copy-done.1
  53.5 0.0 copy-done.2
  53.5 1.3 %multiply_add_fusion = (f32[4,128,256]{2,1,0:T(8,128)}, f32[4,128,256]{2,1,0:T(8,128)}, f32[4,128,256]{2,1,0:T(8,128)}) fusion(f32[4,128,256]{2,1,0:T(8,128)S(1)} %copy-done, f32[4]{0:T(128)S(1)} %get-tuple-element.7, f32[4,128,256]{2,1,0:T(8,128)S(1)} %copy-done.1, f32[4,128,256]{2,1,0:T(8,128)S(1)} %get-tuple-element.6, f32[4]{0:T(128)S(1)} %get-tuple-element.8, ...), kind=kLoop, calls=%fused_computation | loop fusion | flops 786432 | bytes 3670048 | tf_op jit(solution)/shard_map/add | solution.py:515
Async XLA Ops:
  0.6 52.9 %copy-start = (f32[4,128,256]{2,1,0:T(8,128)S(1)}, f32[4,128,256]{2,1,0:T(8,128)}, u32[]{:S(2)}) copy-start(f32[4,128,256]{2,1,0:T(8,128)} %dir_hbm.1) | copy-start | bytes 1572868
  0.6 52.9 %copy-start.1 = (f32[4,128,256]{2,1,0:T(8,128)S(1)}, f32[4,128,256]{2,1,0:T(8,128)}, u32[]{:S(2)}) copy-start(f32[4,128,256]{2,1,0:T(8,128)} %res_hbm.1) | copy-start | bytes 1572868
  0.7 52.9 %copy-start.2 = (f32[4,128,256]{2,1,0:T(8,128)S(1)}, f32[4,128,256]{2,1,0:T(8,128)}, u32[]{:S(2)}) copy-start(f32[4,128,256]{2,1,0:T(8,128)} %param.6) | copy-start | bytes 1572868

commit v4 on v3

--- a/solution.py
+++ b/solution.py
@@ -184,12 +184,12 @@
             high = jnp.maximum(high, pltpu.roll(high, 64, 1))
             high = jnp.maximum(high, pltpu.roll(high, 32, 1))
             table = jnp.where((row == 3) & ((lane >> 5) == b), high, table)
-        t1[0] = table
+        t2[0] = table
 
     pl.semaphore_wait(barrier, nx - 1 + ny - 1)
 
-    for a in range(1, nx):
-        send(t1.at[0], t1.at[a], sem_req.at[0], sem_req.at[1], (lax.rem(tx + a, nx), ty))
+    for b in range(1, ny):
+        send(t2.at[0], t2.at[b], sem_req.at[0], sem_req.at[1], (tx, lax.rem(ty + b, ny)))
 
     columns = jnp.zeros((rows, 128), F32)
     lane_r = lax.broadcasted_iota(jnp.int32, (rows, 128), 1)
@@ -228,10 +228,42 @@
             summed = summed + tables[i]
         return jnp.where(row < CAP, asked, jnp.where(row == CAP, high, summed))
 
-    drain(t1.at[pl.ds(1, nx - 1)], sem_req.at[1])
-    t2[0] = combine(t1, lane // ny, nx)
-    for b in range(1, ny):
-        send(t2.at[0], t2.at[b], sem_req.at[2], sem_req.at[3], (tx, lax.rem(ty + b, ny)))
+    def serve(which, start, stop):
+        def group(g, carry):
+            for i in range(GROUP):
+                k = g * GROUP + i
+                for r in range(CAP):
+                    sb[k, r] = own[jnp.clip(want_s[which, r, k], 0, own.shape[0] - 1)]
+
+                def far():
+                    send(sb.at[k], fetched.at[k], sem_send.at[0], sem_dir.at[g], behind(g, i))
+
+                def near():
+                    pltpu.make_async_copy(sb.at[k], fetched.at[k], sem_dir.at[g]).start()
+
+                if i == 0:
+                    pl.when(g == 0)(near)
+                    pl.when(g > 0)(far)
+                else:
+                    far()
+            return carry
+
+        lax.fori_loop(start, stop, group, 0)
+
+    def wanted(which, asked):
+        want_v[which] = jnp.maximum(asked, 0.0).astype(jnp.int32)
+        copy = pltpu.make_async_copy(want_v.at[which], want_s.at[which], sem_loc.at[1])
+        copy.start()
+        copy.wait()
+
+    early = ny // GROUP
+    drain(t2.at[pl.ds(1, ny - 1)], sem_req.at[1])
+    t1[0] = combine(t2, lax.rem(lane, ny), ny)
+    for a in range(1, nx):
+        send(t1.at[0], t1.at[a], sem_req.at[2], sem_req.at[3], (lax.rem(tx + a, nx), ty))
+    if early:
+        wanted(0, t1[0])
+        serve(0, 0, early)
     with jax.named_scope("laplace"):
         for i in range(2):
             drain(hrin.at[i], sem_halo.at[i])
@@ -252,35 +284,10 @@
             east = jnp.where(col_f == cols - 1, side[:rows, b : b + 1], pltpu.roll(d, cols - 1, 1))
             image_ref[b] = SMOOTH * (4.0 * d - (down + up + east + west))
 
-    drain(t2.at[pl.ds(1, ny - 1)], sem_req.at[3])
-    table = combine(t2, lax.rem(lane, ny), ny)
-    want_v[...] = jnp.maximum(table, 0.0).astype(jnp.int32)
-    want_copy = pltpu.make_async_copy(want_v, want_s, sem_loc.at[1])
-    want_copy.start()
-    want_copy.wait()
-
-    with jax.named_scope("serve"):
-
-        def serve(g, carry):
-            for i in range(GROUP):
-                k = g * GROUP + i
-                for r in range(CAP):
-                    sb[k, r] = own[jnp.clip(want_s[r, k], 0, own.shape[0] - 1)]
-
-                def far():
-                    send(sb.at[k], fetched.at[k], sem_send.at[0], sem_dir.at[g], behind(g, i))
-
-                def near():
-                    pltpu.make_async_copy(sb.at[k], fetched.at[k], sem_dir.at[g]).start()
-
-                if i == 0:
-                    pl.when(g == 0)(near)
-                    pl.when(g > 0)(far)
-                else:
-                    far()
-            return carry
-
-        lax.fori_loop(0, groups, serve, 0)
+    drain(t1.at[pl.ds(1, nx - 1)], sem_req.at[3])
+    table = combine(t1, lane // ny, nx)
+    wanted(1, table)
+    serve(1, early, groups)
 
     bins_copy.wait()
     blocks_copy.wait()
@@ -435,8 +442,8 @@
         beta = norm_new / norm_old
         coef_ref[...] = jnp.where(row < 4, alpha, pltpu.roll(beta, 4, 0))
 
-    drain(t1.at[pl.ds(1, nx - 1)], sem_req.at[0])
-    drain(t2.at[pl.ds(1, ny - 1)], sem_req.at[2])
+    drain(t2.at[pl.ds(1, ny - 1)], sem_req.at[0])
+    drain(t1.at[pl.ds(1, nx - 1)], sem_req.at[2])
     for i in range(2):
         drain(hr, sem_halo.at[4 + i])
         drain(hc, sem_halo.at[6 + i])
@@ -481,10 +488,10 @@
             pltpu.VMEM((8, 128), F32),
             pltpu.VMEM((2, 8, 128), F32),
             pltpu.VMEM((8, 128), jnp.int32),
-            pltpu.VMEM((8, 128), jnp.int32),
+            pltpu.VMEM((2, 8, 128), jnp.int32),
             pltpu.VMEM((n, 128), F32),
             pltpu.SMEM((8, 128), jnp.int32),
-            pltpu.SMEM((8, 128), jnp.int32),
+            pltpu.SMEM((2, 8, 128), jnp.int32),
             pltpu.SemaphoreType.DMA,
             pltpu.SemaphoreType.DMA((6,)),
             pltpu.SemaphoreType.DMA((4,)),

time: 54.9 us -> 54.1 us (0.985)
  Pallas kernels: 52.7 us -> 51.8 us
    pallas_call x1, Pallas kernels: 52.7 us -> 51.8 us  [per_device(): pl.pallas_call(functools.partial(kernel, nx, ny), out_shape=(jax.ShapeDty...]
where the time goes in v4:
time: 54.1 us; the launch traced here: 54 us
  Pallas kernels  51.8 us (96%)
  other arithmetic  1.31 us (2%)
  between operations  0.69 us (1%)
    pallas_call x1, Pallas kernels, per_device(): pl.pallas_call(functools.partial(kernel, nx, ny), out_shape=(jax.ShapeDty...  51.8 us
    add x1, other arithmetic, per_device(): next_direction = next_residual + beta * direction  1.31 us

profile of v4, /device:TPU:1, one launch (start us, length us, event | category | flops | bytes accessed | tf_op | source)
XLA Modules:
  0.0 54.0 jit_solution(3614882035120289047)
XLA Ops:
  0.6 0.0 copy-start
  0.6 0.0 copy-start.1
  0.7 0.0 copy-start.2
  0.7 51.8 %radio_map.1 = (f32[4,128,256]{2,1,0:T(8,128)S(1)}, f32[8,128]{1,0:T(8,128)S(1)}) custom-call(s32[1,256]{1,0:T(1,128)} %bitcast.2, s32[1,256]{1,0:T(1,128)} %bitcast.3, f32[4,128,256]{2,1,0:T(8,128)} %dir_hbm.1, f32[4,128,256]{2,1,0:T(8,128)} %res_hbm.1, bf16[256,128,256]{2,1,0:T(8,128)(2,1)} %blocks_ref.1), custom_call_target="tpu_custom_call" | custom-call | flops 134217728 | bytes 16777216 | tf_op jit(solution)/shard_map/radio_map/pallas_call | solution.py:462
  52.5 0.1 slice_reduce_fusion
  52.7 0.0 copy-done
  52.7 0.0 copy-done.1
  52.7 0.0 copy-done.2
  52.7 1.3 %multiply_add_fusion = (f32[4,128,256]{2,1,0:T(8,128)}, f32[4,128,256]{2,1,0:T(8,128)}, f32[4,128,256]{2,1,0:T(8,128)}) fusion(f32[4,128,256]{2,1,0:T(8,128)S(1)} %copy-done, f32[4]{0:T(128)S(1)} %get-tuple-element.7, f32[4,128,256]{2,1,0:T(8,128)S(1)} %copy-done.1, f32[4,128,256]{2,1,0:T(8,128)S(1)} %get-tuple-element.6, f32[4]{0:T(128)S(1)} %get-tuple-element.8, ...), kind=kLoop, calls=%fused_computation | loop fusion | flops 786432 | bytes 3670048 | tf_op jit(solution)/shard_map/add | solution.py:522
Async XLA Ops:
  0.6 52.0 %copy-start = (f32[4,128,256]{2,1,0:T(8,128)S(1)}, f32[4,128,256]{2,1,0:T(8,128)}, u32[]{:S(2)}) copy-start(f32[4,128,256]{2,1,0:T(8,128)} %dir_hbm.1) | copy-start | bytes 1572868
  0.6 52.0 %copy-start.1 = (f32[4,128,256]{2,1,0:T(8,128)S(1)}, f32[4,128,256]{2,1,0:T(8,128)}, u32[]{:S(2)}) copy-start(f32[4,128,256]{2,1,0:T(8,128)} %res_hbm.1) | copy-start | bytes 1572868
  0.7 52.0 %copy-start.2 = (f32[4,128,256]{2,1,0:T(8,128)S(1)}, f32[4,128,256]{2,1,0:T(8,128)}, u32[]{:S(2)}) copy-start(f32[4,128,256]{2,1,0:T(8,128)} %param.6) | copy-start | bytes 1572868
